TPU v7x, 512 devices: a whole 4x8x8 slice. The times are simulated.
512 devices in a mesh: seq: 64 (over z, y), head: 8 (over x, core).
Axes of the slice: x: 4, y: 8, z: 8, core: 2. Of those that a mesh axis runs over, the one named last changes fastest.
Arguments:
- raw_keys: bfloat16 [2, 65536, 8, 128], P(None, 'seq', 'head'), may hold values from -6 to 6
- raw_values: bfloat16 [2, 65536, 8, 128], P(None, 'seq', 'head'), may hold values from -6 to 6
- phase: int32 [2], replicated, may hold values from 0 to 255, as said below
- ratio: int32 [2, 64], replicated, may hold values from 8 to 32, as said below
- resident_len: int32 [2, 64], replicated, may hold values from 1 to 256, as said below
- beacon_queries: bfloat16 [2, 8192, 8, 8, 128], P(None, 'seq', 'head'), may hold values from -150 to 150
- beacon_wk: bfloat16 [8192, 1024], P('seq', 'head'), may hold values from -0.125 to 0.125
- beacon_wv: bfloat16 [8192, 1024], P('seq', 'head'), may hold values from -0.125 to 0.125
- resident_keys: bfloat16 [2, 16384, 8, 128], P(None, 'seq', 'head'), may hold values from -6 to 6
- resident_values: bfloat16 [2, 16384, 8, 128], P(None, 'seq', 'head'), may hold values from -6 to 6
- decode_queries: bfloat16 [4, 2, 8, 8, 128], P(None, None, 'head'), may hold values from -150 to 150
- out_weight: bfloat16 [8192, 8192], P('head', 'seq'), may hold values from -0.0625 to 0.0625
Outputs:
- beacon_keys: bfloat16 [2, 8192, 8, 128], P(None, 'seq', 'head')
- beacon_values: bfloat16 [2, 8192, 8, 128], P(None, 'seq', 'head')
- projected: bfloat16 [4, 2, 8192], P(None, None, 'seq')
Inputs may be any that keep to these rules, and one draw needn't show every extreme that they name: `phase`: some request has 255. `ratio`: each value is 1024 // 128 times 1, 2 or 4; both ends occur. `resident_len`: some pair has 256.
All inputs are finite; a program needn't handle non-finite values.
Results may differ from a plain program's by a relative error of at most 0.025.
Values may be sent and summed in bfloat16 or wider, within the bound.
No kernel may reach another device: no remote copies, remote signals or barrier semaphores. Data moves between devices by JAX's collectives and lax.ppermute only.
A program may use at most 64 MiB of HBM per device.

v0:
```python
import math
import jax
import jax.numpy as jnp
from jax import lax
from jax.sharding import PartitionSpec as P

G = 8
INTERVAL = 1024
NB = 128
OFF = 256
STEPS = 4
masked_score = -1e30


def shifted(value, axis, steps):
    count = lax.axis_size(axis)
    first, last = (max(0, -steps), min(count, count - steps))
    return lax.ppermute(value, axis, [(source, source + steps) for source in range(first, last)])


def pool_part(queries, key_rows, value_rows, positions, present, reaches):
    inv_root = 1.0 / math.sqrt(queries.shape[-1])

    def per_request(members):
        query_block, key_block, value_block, position_row, present_row, reach_row = members
        scores = (
            jnp.einsum("jkgd,ikd->jkgi", query_block, key_block, preferred_element_type=jnp.float32)
            * inv_root
        )
        allowed = (
            present_row[None, :]
            & (position_row[None, :] >= 0)
            & (position_row[None, :] < INTERVAL)
            & (position_row[None, :] < reach_row[:, None])
        )
        cache_mask = allowed[:, None, None, :]
        row_peak = jnp.max(jnp.where(cache_mask, scores, masked_score), axis=-1)
        weights = jnp.where(cache_mask, jnp.exp(scores - row_peak[..., None]), 0.0)
        weight_sum = jnp.sum(weights, axis=-1)
        weighted = jnp.einsum(
            "jkgi,ikd->jkgd",
            weights.astype(jnp.bfloat16),
            value_block,
            preferred_element_type=jnp.float32,
        )
        return (row_peak, weight_sum, weighted)

    return lax.map(per_request, (queries, key_rows, value_rows, positions, present, reaches))


def body(
    raw_keys,
    raw_values,
    phase,
    ratio,
    resident_len,
    beacon_queries,
    beacon_wk,
    beacon_wv,
    resident_keys,
    resident_values,
    decode_queries,
    out_weight,
):
    requests = raw_keys.shape[0]
    kv_local = raw_keys.shape[2]
    head_dim = raw_keys.shape[3]
    shard_index = lax.axis_index("seq")
    shard_count = lax.axis_size("seq")
    is_first = shard_index == 0
    is_last = shard_index == shard_count - 1
    own_ratio = lax.dynamic_index_in_dim(ratio, shard_index, 1, keepdims=False)
    slot_ids = jnp.arange(NB, dtype=jnp.int32)
    lead_in = jnp.where(is_first, phase, 0)
    reaches = (slot_ids[None, :] + 1) * own_ratio[:, None] + lead_in[:, None]
    tail_keys = raw_keys[:, INTERVAL - OFF :]
    tail_values = raw_values[:, INTERVAL - OFF :]
    own_positions = jnp.arange(INTERVAL, dtype=jnp.int32)[None, :] + phase[:, None]
    rim_ids = jnp.arange(OFF, dtype=jnp.int32)
    rim_positions = rim_ids[None, :] - OFF + phase[:, None]
    near_keys, near_values = shifted((tail_keys, tail_values), "seq", 1)
    key_rows = jnp.concatenate([near_keys, raw_keys], axis=1)
    value_rows = jnp.concatenate([near_values, raw_values], axis=1)
    positions = jnp.concatenate([rim_positions, own_positions], axis=1)
    present = jnp.logical_not(is_first) | (positions >= phase[:, None])
    pooled_parts = pool_part(beacon_queries, key_rows, value_rows, positions, present, reaches)
    pooled = (pooled_parts[2] / pooled_parts[1][..., None]).astype(jnp.bfloat16)
    pooled_flat = pooled.reshape(requests * NB, kv_local * G * head_dim)
    pooled_whole = lax.all_gather(pooled_flat, "head", axis=1, tiled=True)
    key_sum = jnp.dot(
        pooled_whole,
        lax.all_gather(beacon_wk, "seq", axis=0, tiled=True),
        preferred_element_type=jnp.float32,
    )
    value_sum = jnp.dot(
        pooled_whole,
        lax.all_gather(beacon_wv, "seq", axis=0, tiled=True),
        preferred_element_type=jnp.float32,
    )
    made_keys = key_sum
    made_values = value_sum
    made_keys = made_keys.reshape(requests, NB, kv_local, head_dim)
    made_values = made_values.reshape(requests, NB, kv_local, head_dim)
    slot_live = slot_ids[None, :] < (INTERVAL // own_ratio)[:, None]
    beacon_keys = jnp.where(slot_live[:, :, None, None], made_keys, 0.0).astype(jnp.bfloat16)
    beacon_values = jnp.where(slot_live[:, :, None, None], made_values, 0.0).astype(jnp.bfloat16)
    cache_keys = jnp.concatenate([resident_keys, beacon_keys, tail_keys], axis=1)
    cache_values = jnp.concatenate([resident_values, beacon_values, tail_values], axis=1)
    own_len = lax.dynamic_index_in_dim(resident_len, shard_index, 1, keepdims=False)
    resident_ok = jnp.arange(resident_keys.shape[1], dtype=jnp.int32)[None, :] < own_len[:, None]
    leftover_ok = (rim_ids[None, :] >= OFF - phase[:, None]) & is_last
    usable = jnp.concatenate([resident_ok, slot_live, leftover_ok], axis=1)
    inv_root = 1.0 / math.sqrt(head_dim)
    scores = (
        jnp.einsum(
            "srkgd,rikd->rksgi", decode_queries, cache_keys, preferred_element_type=jnp.float32
        )
        * inv_root
    )
    cache_mask = usable[:, None, None, None, :]
    row_peak = jnp.max(jnp.where(cache_mask, scores, masked_score), axis=-1)
    weights = jnp.where(cache_mask, jnp.exp(scores - row_peak[..., None]), 0.0)
    weight_sum = jnp.sum(weights, axis=-1)
    weighted = jnp.einsum(
        "rksgi,rikd->rksgd",
        weights.astype(jnp.bfloat16),
        cache_values,
        preferred_element_type=jnp.float32,
    )
    global_peak = lax.pmax(row_peak, "seq")
    rescale = jnp.exp(row_peak - global_peak)
    total_sum, total_weighted = lax.psum(
        (weight_sum * rescale, weighted * rescale[..., None]), "seq"
    )
    attended = (total_weighted / total_sum[..., None]).astype(jnp.bfloat16)
    attended = jnp.transpose(attended, (2, 0, 1, 3, 4)).reshape(
        STEPS * requests, kv_local * G * head_dim
    )
    partial_value = jnp.dot(attended, out_weight, preferred_element_type=jnp.float32)
    summed = lax.psum(partial_value, "head")
    projected = summed.astype(jnp.bfloat16).reshape(STEPS, requests, out_weight.shape[1])
    return (beacon_keys, beacon_values, projected)


def solution(mesh):
    return jax.shard_map(
        body,
        mesh=mesh,
        in_specs=(
            P(None, "seq", "head", None),
            P(None, "seq", "head", None),
            P(),
            P(),
            P(),
            P(None, "seq", "head", None, None),
            P("seq", "head"),
            P("seq", "head"),
            P(None, "seq", "head", None),
            P(None, "seq", "head", None),
            P(None, None, "head", None, None),
            P("head", "seq"),
        ),
        out_specs=(
            P(None, "seq", "head", None),
            P(None, "seq", "head", None),
            P(None, None, "seq"),
        ),
        check_vma=False,
    )
```

profile of v0, /device:TPU:1, one launch (start us, length us, event | category | flops | bytes accessed | tf_op | source)
XLA Modules:
  0.0 666.6 jit_solution(5328392180371530264)
XLA Ops:
  7.2 1.0 slice.9
  8.2 4.7 collective-permute-start.1
  12.9 0.9 slice.8
  13.8 2.6 collective-permute-start
  17.9 1.2 copy.32
  20.6 1.0 fusion.44
  21.8 1.1 pad_maximum_fusion
  22.9 1.0 copy.31
  24.8 8.6 %while.12 = (s32[]{:T(128)}, f32[2,128,1,8]{1,3,2,0:T(8,128)S(1)}, f32[2,128,1,8,128]{1,4,3,2,0:T(8,128)S(1)}, pred[2,1280]{1,0:T(4,128)(4,1)S(1)}, s32[2,1280]{...) while((s32[]{:T(128)}, f32[2,128,1,8]{1,3,2,0:T(8,128)S(1)}, ...), condition=%wide.region_3.4_spmd, body=%wide.region_0.3_spmd.sunk | while | flops 685837312 | bytes 21023128 | solution.py:48
  24.9 0.9 compare_and_fusion.3
  26.8 1.2 fusion.67
  27.9 1.1 fusion.66
  29.2 0.9 compare_and_fusion.3
  31.1 1.2 fusion.67
  32.3 1.1 fusion.66
  33.8 0.9 copy.60
  35.8 64.2 %all-gather.6.cloned.1.call-done = bf16[8192,128]{1,0:T(8,128)(2,1)} async-done(((bf16[128,128]{1,0:T(8,128)(2,1)}), bf16[8192,128]{1,0:T(8,128)(2,1)}) %all-gather.6.cloned.1.call-update) | async-done | bytes 2097168 | tf_op jit(solution)/shard_map/all_gather | solution.py:92
  99.9 40.7 %all-gather.4.cloned.1.call-done = bf16[256,8192]{1,0:T(8,128)(2,1)} async-done(((bf16[256,1024]{1,0:T(8,128)(2,1)}), bf16[256,8192]{1,0:T(8,128)(2,1)}) %all-gather.4.cloned.1.call-update) | async-done | bytes 4194320 | tf_op jit(solution)/shard_map/all_gather | solution.py:89
  140.6 4.1 fusion.48
  144.8 78.4 %all-gather.8.cloned.1.call-done = bf16[8192,128]{1,0:T(8,128)(2,1)} async-done(((bf16[128,128]{1,0:T(8,128)(2,1)}), bf16[8192,128]{1,0:T(8,128)(2,1)}) %all-gather.8.cloned.1.call-update) | async-done | bytes 2097168 | tf_op jit(solution)/shard_map/all_gather | solution.py:97
  223.1 4.1 fusion.49
  227.9 113.3 %pmax.7 = f32[2,1,4,8]{3,2,0,1:T(4,128)S(1)} all-reduce(f32[2,1,4,8]{3,2,0,1:T(4,128)S(1)} %bitcast.153), channel_id=1, replica_groups=mesh['seq'=64,'head'=8] {'seq'}, use_global_device_ids=true, to_apply=%region_5.6 | all-reduce | flops 64 | bytes 512 | tf_op jit(solution)/shard_map/pmax | solution.py:130
  341.5 219.7 %all-reduce = (f32[2,1,4,8,128]{4,3,2,0,1:T(8,128)S(1)}, f32[2,4,8]{2,1,0:T(4,128)S(1)}) all-reduce(f32[2,1,4,8,128]{4,3,2,0,1:T(8,128)S(1)} %fusion.25, f32[2,4,8]{2,1,0:T(4,128)S(1)} %get-tuple-element.101), channel_id=1, replica_groups=mesh['seq'=64,'head'=8] {'seq'}, use_global_device_ids=true, to_apply=%region_6.7 | all-reduce | flops 8256 | bytes 66048 | tf_op jit(solution)/shard_map/psum | solution.py:132
  561.5 98.6 %psum.23 = bf16[8,128]{1,0:T(8,128)(2,1)} all-reduce(f32[8,128]{1,0:T(8,128)S(1)} %fusion.37), channel_id=1, replica_groups=mesh['seq'=64,'head'=8] {'head'}, use_global_device_ids=true, to_apply=%region_9.10 | all-reduce | flops 1024 | bytes 6144 | tf_op jit(solution)/shard_map/psum | solution.py:140
  (63 shorter events, 8.5 us)
Async XLA Ops:
  7.2 554.2 %copy-start = (bf16[1024,128]{1,0:T(8,128)(2,1)S(1)}, bf16[1024,128]{1,0:T(8,128)(2,1)}, u32[]{:S(2)}) copy-start(bf16[1024,128]{1,0:T(8,128)(2,1)} %param.25) | copy-start | bytes 786436
  7.2 17.6 %copy-start.1 = (bf16[2,128,1,8,128]{4,3,2,1,0:T(8,128)(2,1)S(1)}, bf16[2,128,1,8,128]{4,3,2,1,0:T(8,128)(2,1)}, u32[]{:S(2)}) copy-start(bf16[2,128,1,8,128]{4,3,2,1,0:T(8,128)(2,1)} %param.19) | copy-start | bytes 1572868
  7.2 92.7 %all-gather.6.cloned.1.call-start = ((), (), s32[]{:S(2)}) async-start(), calls=%async_computation.1 | async-start | bytes 2129920 | tf_op jit(solution)/shard_map/all_gather | solution.py:92
  8.2 14.6 %collective-permute-start.1 = (bf16[2,256,1,128]{3,1,0,2:T(8,128)(2,1)S(1)}, bf16[2,256,1,128]{3,1,0,2:T(8,128)(2,1)}, u32[]{:S(2)}, u32[]{:S(2)}) collective-permute-start(bf16[2,256,1,128]{3,1,0,2:T(8,128)(2,1)S(1)} %slice.9), channel_id=1, source_target_pairs={{0,8},{8,16},{16,24},{24,32},{32,40},{40,48},{48,56},{56,64},{64,7... | collective-permute-start | bytes 393224 | tf_op jit(solution)/shard_map/ppermute | solution.py:18
  13.8 7.9 %collective-permute-start = (bf16[2,256,1,128]{3,1,0,2:T(8,128)(2,1)S(1)}, bf16[2,256,1,128]{3,1,0,2:T(8,128)(2,1)S(1)}, u32[]{:S(2)}, u32[]{:S(2)}) collective-permute-start(bf16[2,256,1,128]{3,1,0,2:T(8,128)(2,1)S(1)} %slice.8), channel_id=1, source_target_pairs={{0,8},{8,16},{16,24},{24,32},{32,40},{40,48},{48,56},{56,64},{64,7... | collective-permute-start | bytes 393224 | tf_op jit(solution)/shard_map/ppermute | solution.py:18
  16.4 124.2 %all-gather.4.cloned.1.call-start = ((), (), s32[]{:S(2)}) async-start(), calls=%async_computation | async-start | bytes 4718592 | tf_op jit(solution)/shard_map/all_gather | solution.py:89
  24.8 2.0 copy-start.2
  29.1 2.0 copy-start.2
  34.8 188.4 %all-gather.8.cloned.1.call-start = ((), (), s32[]{:S(2)}) async-start(), calls=%async_computation.2 | async-start | bytes 2129920 | tf_op jit(solution)/shard_map/all_gather | solution.py:97
  144.7 82.6 %copy-start.5 = (bf16[2,256,1,128]{3,1,2,0:T(8,128)(2,1)S(1)}, bf16[2,256,1,128]{3,1,2,0:T(8,128)(2,1)}, u32[]{:S(2)}) copy-start(bf16[2,256,1,128]{3,1,2,0:T(8,128)(2,1)} %param.22) | copy-start | bytes 393220
  144.8 82.6 %copy-start.7 = (bf16[4,2,1,8,128]{4,3,2,1,0:T(8,128)(2,1)S(1)}, bf16[4,2,1,8,128]{4,3,2,1,0:T(8,128)(2,1)}, u32[]{:S(2)}) copy-start(bf16[4,2,1,8,128]{4,3,2,1,0:T(8,128)(2,1)} %param.24) | copy-start | bytes 49156
  144.8 196.5 %copy-start.6 = (bf16[2,256,1,128]{3,1,2,0:T(8,128)(2,1)S(1)}, bf16[2,256,1,128]{3,1,2,0:T(8,128)(2,1)}, u32[]{:S(2)}) copy-start(bf16[2,256,1,128]{3,1,2,0:T(8,128)(2,1)} %param.23) | copy-start | bytes 393220
  227.4 432.7 %copy-start.3 = (bf16[2,128,1,128]{3,1,0,2:T(8,128)(2,1)}, bf16[2,128,1,128]{3,1,0,2:T(8,128)(2,1)S(1)}, u32[]{:S(2)}) copy-start(bf16[2,128,1,128]{3,1,0,2:T(8,128)(2,1)S(1)} %get-tuple-element.105) | copy-start | bytes 196612
  227.4 432.7 %copy-start.4 = (bf16[2,128,1,128]{3,1,0,2:T(8,128)(2,1)}, bf16[2,128,1,128]{3,1,0,2:T(8,128)(2,1)S(1)}, u32[]{:S(2)}) copy-start(bf16[2,128,1,128]{3,1,0,2:T(8,128)(2,1)S(1)} %get-tuple-element.106) | copy-start | bytes 196612
Sparse Core Ops, SparseCore 0:
  16.6 83.3 all-gather.5
  102.0 38.5 all-gather.3
  143.7 79.3 all-gather.7
where the time goes:
time: 667 us
  blocking collectives  432 us (65%)
  waiting for transfers between devices  184 us (28%)
  between operations  14 us (2%)
  matrix products  13.1 us (2%)
  other arithmetic  10.8 us (2%)
  starting transfers between devices  7.38 us (1%)
    psum x1, blocking collectives, body(): lax.psum((weight_sum * rescale, weighted * rescale[..., None]), 'seq')  220 us
    pmax x1, blocking collectives, body(): global_peak = lax.pmax(row_peak, 'seq')  113 us
    psum x1, blocking collectives, body(): summed = lax.psum(partial_value, 'head')  98.6 us
    all_gather x1, waiting for transfers between devices, body(): lax.all_gather(beacon_wv, 'seq', axis=0, tiled=True)  78.4 us
    all_gather x1, waiting for transfers between devices, body(): lax.all_gather(beacon_wk, 'seq', axis=0, tiled=True)  64.2 us
    all_gather x1, waiting for transfers between devices, body(): pooled_whole = lax.all_gather(pooled_flat, 'head', axis=1, tiled=True)  40.7 us
  transfers between devices with their start and end apart: 5, of which 3 were waited for; matrix products, arithmetic and copies ran while one was open for 3% of the time, Pallas kernels for 0%

commit v1 on v0

--- a/solution.py
+++ b/solution.py
@@ -86,7 +86,12 @@
     pooled_parts = pool_part(beacon_queries, key_rows, value_rows, positions, present, reaches)
     pooled = (pooled_parts[2] / pooled_parts[1][..., None]).astype(jnp.bfloat16)
     pooled_flat = pooled.reshape(requests * NB, kv_local * G * head_dim)
-    pooled_whole = lax.all_gather(pooled_flat, "head", axis=1, tiled=True)
+    ring = [pooled_flat]
+    for hop in range(7):
+        ring.append(lax.ppermute(ring[-1], "head", [(dev, (dev + 1) % 8) for dev in range(8)]))
+    pooled_whole = jnp.roll(
+        jnp.concatenate(ring[::-1], axis=1), (lax.axis_index("head") + 1) * ring[0].shape[1], axis=1
+    )
     key_sum = jnp.dot(
         pooled_whole,
         lax.all_gather(beacon_wk, "seq", axis=0, tiled=True),

time: 667 us -> 628 us (0.942)
  waiting for transfers between devices: 184 us -> 113 us
  starting transfers between devices: 7.38 us -> 23.3 us
  local copies, waits for them, and re-layouts: 5.63 us -> 21.4 us
    all_gather x1, waiting for transfers between devices: 64.2 us -> 0.01 us  [body(): lax.all_gather(beacon_wk, 'seq', axis=0, tiled=True)]
    ppermute x0 -> x7, waiting for transfers between devices: none -> 46.7 us  [body(): lax.ppermute(ring[-1], 'head', [(dev, (dev + 1) % 8) for dev in range(8)])]
    all_gather x1 -> x0, waiting for transfers between devices: 40.7 us -> none  [body(): pooled_whole = lax.all_gather(pooled_flat, 'head', axis=1, tiled=True)]
    ppermute x0 -> x7, starting transfers between devices: none -> 15.9 us  [body(): lax.ppermute(ring[-1], 'head', [(dev, (dev + 1) % 8) for dev in range(8)])]
    unnamed x16 -> x33, local copies, waits for them, and re-layouts: 2.24 us -> 16.2 us
    all_gather x1, waiting for transfers between devices: 78.4 us -> 66.7 us  [body(): lax.all_gather(beacon_wv, 'seq', axis=0, tiled=True)]
  transfers between devices with their start and end apart: 5 -> 11, of which waited for: 3 -> 8; matrix products, arithmetic and copies ran while one was open for 3% -> 6% of each run, Pallas kernels for 0% -> 0%
where the time goes in v1:
time: 628 us; the launch traced here: 627 us
  blocking collectives  432 us (69%)
  waiting for transfers between devices  113 us (18%)
  starting transfers between devices  23.3 us (4%)
  local copies, waits for them, and re-layouts  21.4 us (3%)
  between operations  14.3 us (2%)
  matrix products  13.1 us (2%)
  other arithmetic  9.99 us (2%)
    psum x1, blocking collectives, body(): lax.psum((weight_sum * rescale, weighted * rescale[..., None]), 'seq')  220 us
    pmax x1, blocking collectives, body(): global_peak = lax.pmax(row_peak, 'seq')  113 us
    psum x1, blocking collectives, body(): summed = lax.psum(partial_value, 'head')  98.6 us
    all_gather x1, waiting for transfers between devices, body(): lax.all_gather(beacon_wv, 'seq', axis=0, tiled=True)  66.7 us
    ppermute x7, waiting for transfers between devices, body(): lax.ppermute(ring[-1], 'head', [(dev, (dev + 1) % 8) for dev in range(8)])  46.7 us
    unnamed x33, local copies, waits for them, and re-layouts  16.2 us
    ppermute x7, starting transfers between devices, body(): lax.ppermute(ring[-1], 'head', [(dev, (dev + 1) % 8) for dev in range(8)])  15.9 us
  transfers between devices with their start and end apart: 11, of which 8 were waited for; matrix products, arithmetic and copies ran while one was open for 6% of the time, Pallas kernels for 0%

profile of v1, /device:TPU:1, one launch (start us, length us, event | category | flops | bytes accessed | tf_op | source)
XLA Modules:
  0.0 627.2 jit_solution(12281752857547268177)
XLA Ops:
  8.2 4.0 collective-permute-start.1
  13.2 3.2 collective-permute-start
  23.0 10.5 %while.12 = (s32[]{:T(128)}, f32[2,128,1,8]{1,3,2,0:T(8,128)S(1)}, f32[2,128,1,8,128]{1,4,3,2,0:T(8,128)S(1)}, pred[2,1280]{1,0:T(4,128)(4,1)S(1)}, s32[2,1280]{...) while((s32[]{:T(128)}, f32[2,128,1,8]{1,3,2,0:T(8,128)S(1)}, ...), condition=%wide.region_3.4_spmd, body=%wide.region_0.3_spmd.sunk | while | flops 685837312 | bytes 18401660 | solution.py:48
  34.0 2.3 collective-permute-start.2
  36.4 6.1 collective-permute-done.2
  42.5 2.5 collective-permute-start.3
  45.0 6.1 collective-permute-done.3
  51.1 2.5 collective-permute-start.4
  53.6 6.1 collective-permute-done.4
  59.7 2.5 collective-permute-start.5
  62.2 6.1 collective-permute-done.5
  68.3 2.5 collective-permute-start.6
  70.8 6.1 collective-permute-done.6
  76.9 2.5 collective-permute-start.7
  79.5 7.4 %collective-permute-done.7 = bf16[256,1024]{1,0:T(8,128)(2,1)} collective-permute-done((bf16[256,1024]{1,0:T(8,128)(2,1)S(1)}, bf16[256,1024]{1,0:T(8,128)(2,1)}, u32[]{:S(2)}, u32[]{:S(2)}) %collective-permute-start.7) | collective-permute-done | bytes 524320 | tf_op jit(solution)/shard_map/ppermute | solution.py:91
  88.3 8.6 %collective-permute-done.8 = bf16[256,1024]{1,0:T(8,128)(2,1)S(1)} collective-permute-done((bf16[256,1024]{1,0:T(8,128)(2,1)}, bf16[256,1024]{1,0:T(8,128)(2,1)S(1)}, u32[]{:S(2)}, u32[]{:S(2)}) %collective-permute-start.8) | collective-permute-done | bytes 524320 | tf_op jit(solution)/shard_map/ppermute | solution.py:91
  97.8 1.9 constant_dynamic-update-slice_fusion.14
  105.6 1.9 constant_dynamic-update-slice_fusion.6
  112.6 4.1 fusion.27
  116.7 66.7 %all-gather.5.cloned.1.call-done = bf16[8192,128]{1,0:T(8,128)(2,1)} async-done(((bf16[128,128]{1,0:T(8,128)(2,1)}), bf16[8192,128]{1,0:T(8,128)(2,1)}) %all-gather.5.cloned.1.call-update) | async-done | bytes 2097168 | tf_op jit(solution)/shard_map/all_gather | solution.py:102
  183.4 4.1 fusion.25
  188.2 113.3 %pmax.7 = f32[2,1,4,8]{3,2,0,1:T(4,128)S(1)} all-reduce(f32[2,1,4,8]{3,2,0,1:T(4,128)S(1)} %bitcast.157), channel_id=1, replica_groups=mesh['seq'=64,'head'=8] {'seq'}, use_global_device_ids=true, to_apply=%region_5.6 | all-reduce | flops 64 | bytes 512 | tf_op jit(solution)/shard_map/pmax | solution.py:135
  301.8 219.7 %all-reduce = (f32[2,1,4,8,128]{4,3,2,0,1:T(8,128)S(1)}, f32[2,4,8]{2,1,0:T(4,128)S(1)}) all-reduce(f32[2,1,4,8,128]{4,3,2,0,1:T(8,128)S(1)} %fusion.29, f32[2,4,8]{2,1,0:T(4,128)S(1)} %get-tuple-element.101), channel_id=1, replica_groups=mesh['seq'=64,'head'=8] {'seq'}, use_global_device_ids=true, to_apply=%region_6.7 | all-reduce | flops 8256 | bytes 66048 | tf_op jit(solution)/shard_map/psum | solution.py:137
  521.8 98.6 %psum.23 = bf16[8,128]{1,0:T(8,128)(2,1)} all-reduce(f32[8,128]{1,0:T(8,128)S(1)} %fusion.41), channel_id=1, replica_groups=mesh['seq'=64,'head'=8] {'head'}, use_global_device_ids=true, to_apply=%region_9.10 | all-reduce | flops 1024 | bytes 6144 | tf_op jit(solution)/shard_map/psum | solution.py:145
  (88 shorter events, 33.8 us)
Async XLA Ops:
  7.2 514.4 %copy-start = (bf16[1024,128]{1,0:T(8,128)(2,1)S(1)}, bf16[1024,128]{1,0:T(8,128)(2,1)}, u32[]{:S(2)}) copy-start(bf16[1024,128]{1,0:T(8,128)(2,1)} %param.25) | copy-start | bytes 786436
  7.2 105.5 %all-gather.3.cloned.1.call-start = ((), (), s32[]{:S(2)}) async-start(), calls=%async_computation | async-start | bytes 2129920 | tf_op jit(solution)/shard_map/all_gather | solution.py:97
  8.2 14.6 %collective-permute-start.1 = (bf16[2,256,1,128]{3,1,0,2:T(8,128)(2,1)S(1)}, bf16[2,256,1,128]{3,1,0,2:T(8,128)(2,1)S(1)}, u32[]{:S(2)}, u32[]{:S(2)}) collective-permute-start(bf16[2,256,1,128]{3,1,0,2:T(8,128)(2,1)S(1)} %slice.9), channel_id=1, source_target_pairs={{0,8},{8,16},{16,24},{24,32},{32,40},{40,48},{48,56},{56,64},{64,7... | collective-permute-start | bytes 393224 | tf_op jit(solution)/shard_map/ppermute | solution.py:18
  13.2 8.6 %copy-start.1 = (bf16[2,256,1,128]{3,1,0,2:T(8,128)(2,1)}, bf16[2,256,1,128]{3,1,0,2:T(8,128)(2,1)S(1)}, u32[]{:S(2)}) copy-start(bf16[2,256,1,128]{3,1,0,2:T(8,128)(2,1)S(1)} %slice.8) | copy-start | bytes 393220
  13.2 8.6 %collective-permute-start = (bf16[2,256,1,128]{3,1,0,2:T(8,128)(2,1)S(1)}, bf16[2,256,1,128]{3,1,0,2:T(8,128)(2,1)S(1)}, u32[]{:S(2)}, u32[]{:S(2)}) collective-permute-start(bf16[2,256,1,128]{3,1,0,2:T(8,128)(2,1)S(1)} %slice.8), channel_id=1, source_target_pairs={{0,8},{8,16},{16,24},{24,32},{32,40},{40,48},{48,56},{56,64},{64,7... | collective-permute-start | bytes 393224 | tf_op jit(solution)/shard_map/ppermute | solution.py:18
  16.4 167.0 %all-gather.5.cloned.1.call-start = ((), (), s32[]{:S(2)}) async-start(), calls=%async_computation.1 | async-start | bytes 2129920 | tf_op jit(solution)/shard_map/all_gather | solution.py:102
  34.0 8.5 %collective-permute-start.2 = (bf16[256,1024]{1,0:T(8,128)(2,1)S(1)}, bf16[256,1024]{1,0:T(8,128)(2,1)S(1)}, u32[]{:S(2)}, u32[]{:S(2)}) collective-permute-start(bf16[256,1024]{1,0:T(8,128)(2,1)S(1)} %bitcast.150), channel_id=1, source_target_pairs={{0,1},{1,2},{2,3},{3,4},{4,5},{5,6},{6,7},{7,0},{8,9},{9,10},{10,1... | collective-permute-start | bytes 1572872 | tf_op jit(solution)/shard_map/ppermute | solution.py:91
  42.5 8.6 %collective-permute-start.3 = (bf16[256,1024]{1,0:T(8,128)(2,1)S(1)}, bf16[256,1024]{1,0:T(8,128)(2,1)S(1)}, u32[]{:S(2)}, u32[]{:S(2)}) collective-permute-start(bf16[256,1024]{1,0:T(8,128)(2,1)S(1)} %collective-permute-done.2), channel_id=1, source_target_pairs={{0,1},{1,2},{2,3},{3,4},{4,5},{5,6},{6,7},{7,0},{8,9},{9,10},{10,1... | collective-permute-start | bytes 1572872 | tf_op jit(solution)/shard_map/ppermute | solution.py:91
  51.1 8.6 %collective-permute-start.4 = (bf16[256,1024]{1,0:T(8,128)(2,1)S(1)}, bf16[256,1024]{1,0:T(8,128)(2,1)S(1)}, u32[]{:S(2)}, u32[]{:S(2)}) collective-permute-start(bf16[256,1024]{1,0:T(8,128)(2,1)S(1)} %collective-permute-done.3), channel_id=1, source_target_pairs={{0,1},{1,2},{2,3},{3,4},{4,5},{5,6},{6,7},{7,0},{8,9},{9,10},{10,1... | collective-permute-start | bytes 1572872 | tf_op jit(solution)/shard_map/ppermute | solution.py:91
  59.7 8.6 %collective-permute-start.5 = (bf16[256,1024]{1,0:T(8,128)(2,1)S(1)}, bf16[256,1024]{1,0:T(8,128)(2,1)S(1)}, u32[]{:S(2)}, u32[]{:S(2)}) collective-permute-start(bf16[256,1024]{1,0:T(8,128)(2,1)S(1)} %collective-permute-done.4), channel_id=1, source_target_pairs={{0,1},{1,2},{2,3},{3,4},{4,5},{5,6},{6,7},{7,0},{8,9},{9,10},{10,1... | collective-permute-start | bytes 1572872 | tf_op jit(solution)/shard_map/ppermute | solution.py:91
  68.3 8.6 %collective-permute-start.6 = (bf16[256,1024]{1,0:T(8,128)(2,1)S(1)}, bf16[256,1024]{1,0:T(8,128)(2,1)S(1)}, u32[]{:S(2)}, u32[]{:S(2)}) collective-permute-start(bf16[256,1024]{1,0:T(8,128)(2,1)S(1)} %collective-permute-done.5), channel_id=1, source_target_pairs={{0,1},{1,2},{2,3},{3,4},{4,5},{5,6},{6,7},{7,0},{8,9},{9,10},{10,1... | collective-permute-start | bytes 1572872 | tf_op jit(solution)/shard_map/ppermute | solution.py:91
  76.9 9.9 %collective-permute-start.7 = (bf16[256,1024]{1,0:T(8,128)(2,1)S(1)}, bf16[256,1024]{1,0:T(8,128)(2,1)}, u32[]{:S(2)}, u32[]{:S(2)}) collective-permute-start(bf16[256,1024]{1,0:T(8,128)(2,1)S(1)} %collective-permute-done.6), channel_id=1, source_target_pairs={{0,1},{1,2},{2,3},{3,4},{4,5},{5,6},{6,7},{7,0},{8,9},{9,10},{10,1... | collective-permute-start | bytes 1572872 | tf_op jit(solution)/shard_map/ppermute | solution.py:91
  86.9 10.0 %collective-permute-start.8 = (bf16[256,1024]{1,0:T(8,128)(2,1)}, bf16[256,1024]{1,0:T(8,128)(2,1)S(1)}, u32[]{:S(2)}, u32[]{:S(2)}) collective-permute-start(bf16[256,1024]{1,0:T(8,128)(2,1)} %collective-permute-done.7), channel_id=1, source_target_pairs={{0,1},{1,2},{2,3},{3,4},{4,5},{5,6},{6,7},{7,0},{8,9},{9,10},{10,1... | collective-permute-start | bytes 1572872 | tf_op jit(solution)/shard_map/ppermute | solution.py:91
  109.2 78.4 %copy-start.2 = (bf16[2,256,1,128]{3,1,0,2:T(8,128)(2,1)S(1)}, bf16[2,256,1,128]{3,1,0,2:T(8,128)(2,1)}, u32[]{:S(2)}) copy-start(bf16[2,256,1,128]{3,1,0,2:T(8,128)(2,1)} %copy-done.1) | copy-start | bytes 393220
  109.2 78.5 %copy-start.5 = (bf16[2,256,1,128]{3,1,2,0:T(8,128)(2,1)S(1)}, bf16[2,256,1,128]{3,1,2,0:T(8,128)(2,1)}, u32[]{:S(2)}) copy-start(bf16[2,256,1,128]{3,1,2,0:T(8,128)(2,1)} %param.22) | copy-start | bytes 393220
  109.2 78.5 %copy-start.7 = (bf16[4,2,1,8,128]{4,3,2,1,0:T(8,128)(2,1)S(1)}, bf16[4,2,1,8,128]{4,3,2,1,0:T(8,128)(2,1)}, u32[]{:S(2)}) copy-start(bf16[4,2,1,8,128]{4,3,2,1,0:T(8,128)(2,1)} %param.24) | copy-start | bytes 49156
  110.9 190.7 %copy-start.6 = (bf16[2,256,1,128]{3,1,2,0:T(8,128)(2,1)S(1)}, bf16[2,256,1,128]{3,1,2,0:T(8,128)(2,1)}, u32[]{:S(2)}) copy-start(bf16[2,256,1,128]{3,1,2,0:T(8,128)(2,1)} %param.23) | copy-start | bytes 393220
  187.6 432.7 %copy-start.3 = (bf16[2,128,1,128]{3,1,0,2:T(8,128)(2,1)}, bf16[2,128,1,128]{3,1,0,2:T(8,128)(2,1)S(1)}, u32[]{:S(2)}) copy-start(bf16[2,128,1,128]{3,1,0,2:T(8,128)(2,1)S(1)} %get-tuple-element.105) | copy-start | bytes 196612
  187.7 432.7 %copy-start.4 = (bf16[2,128,1,128]{3,1,0,2:T(8,128)(2,1)}, bf16[2,128,1,128]{3,1,0,2:T(8,128)(2,1)S(1)}, u32[]{:S(2)}) copy-start(bf16[2,128,1,128]{3,1,0,2:T(8,128)(2,1)S(1)} %get-tuple-element.106) | copy-start | bytes 196612
Sparse Core Ops, SparseCore 0:
  16.5 83.1 all-gather.2
  102.8 80.5 all-gather.4
